TPU v7x, 32 devices: a whole 2x2x4 slice. The times are simulated.
32 devices in a mesh: seq: 4 (over z), tm: 8 (over y, x, core).
Axes of the slice: x: 2, y: 2, z: 4, core: 2. Of those that a mesh axis runs over, the one named last changes fastest.
Arguments:
- inputs: float32 [4, 2048, 64], P('seq', 'tm'), may hold values from -6 to 6
- guess: float32 [4, 2048, 64], P('seq', 'tm'), may hold values from -0.9 to 0.9
- cotangent: float32 [4, 2048, 64], P('seq', 'tm'), may hold values from -0.4 to 0.4
- w_input: float32 [64, 192], replicated, may hold values from -0.75 to 0.75
- w_hidden: float32 [64, 192], replicated, may hold values from -0.75 to 0.75
- bias: float32 [256], replicated, may hold values from -2 to 13, as said below
Outputs:
- new_states: float32 [4, 2048, 64], P('seq', 'tm')
- adjoint: float32 [4, 2048, 64], P('seq', 'tm')
- grad_input: float32 [64, 192], replicated
- grad_hidden: float32 [64, 192], replicated
- grad_bias: float32 [256], replicated
Inputs may be any that keep to these rules, and one draw needn't show every extreme that they name: `bias`: gate biases as laid out in the meaning.
All inputs are finite; a program needn't handle non-finite values.
Results may differ from a plain program's by a relative error of at most 0.00075.
Values sent between devices are 32-bit elements; how exact they have to be, the bound alone decides.
A program may use at most 128 MiB of HBM per device.

v0:
```python
import math

import jax
import jax.numpy as jnp
from jax import lax
from jax.sharding import PartitionSpec as P

HIGHEST = lax.Precision.HIGHEST


def shifted(x, axis, by):
    count = lax.axis_size(axis)
    pairs = [(i, i + by) for i in range(count) if 0 <= i + by < count]
    return lax.ppermute(x, axis, pairs)


def prefix(value, axis, join, neutral, backward):
    count, mine = (lax.axis_size(axis), lax.axis_index(axis))
    pieces = jax.tree.map(lambda part: lax.all_gather(part, axis), value)
    if backward:
        pieces = jax.tree.map(lambda part: part[::-1], pieces)
        mine = count - 1 - mine
    total = jax.tree.map(
        lambda part, zero: jnp.full_like(part, 0) + jnp.asarray(zero, part.dtype), value, neutral
    )

    def lap(position, total):
        longer = join(total, jax.tree.map(lambda part: part[position], pieces))
        return jax.tree.map(lambda new, old: jnp.where(position < mine, new, old), longer, total)

    return lax.fori_loop(0, count - 1, lap, total)


def cell(inputs, prev, w_input, w_hidden, bias):
    width = prev.shape[-1]
    gate_in = jnp.einsum("...d,dk->...k", inputs, w_input, precision=HIGHEST) + bias[: 3 * width]
    gate_hid = jnp.einsum("...j,jk->...k", prev, w_hidden, precision=HIGHEST)
    reset = jax.nn.sigmoid(gate_in[..., :width] + gate_hid[..., :width])
    update = jax.nn.sigmoid(gate_in[..., width : 2 * width] + gate_hid[..., width : 2 * width])
    hsum = gate_hid[..., 2 * width :] + bias[3 * width :]
    cand = jnp.tanh(gate_in[..., 2 * width :] + reset * hsum)
    value = (1.0 - update) * cand + update * prev
    return (value, (reset, update, cand, hsum))


def jacobian(prev, w_hidden, reset, update, cand, hsum):
    width = prev.shape[-1]
    w_reset = w_hidden[:, :width].T
    w_update = w_hidden[:, width : 2 * width].T
    w_cand = w_hidden[:, 2 * width :].T
    squash = (1.0 - update) * (1.0 - cand * cand)
    coef_cand = squash * reset
    coef_reset = squash * hsum * reset * (1.0 - reset)
    coef_update = (prev - cand) * update * (1.0 - update)
    identity_mat = jnp.eye(width, dtype=jnp.float32)
    return (
        coef_cand[..., :, None] * w_cand
        + coef_reset[..., :, None] * w_reset
        + coef_update[..., :, None] * w_update
        + update[..., :, None] * identity_mat
    )


def compose(earlier, later):
    matrix = jnp.einsum("...ij,...jk->...ik", later[0], earlier[0], precision=HIGHEST)
    offset = jnp.einsum("...ij,...j->...i", later[0], earlier[1], precision=HIGHEST) + later[1]
    return (matrix, offset)


def block_prefix(mats, offs):
    seqs_here, length, width = offs.shape
    run = 16
    groups = length // run
    mats_run = mats.reshape(seqs_here, groups, run, width, width)
    offs_run = offs.reshape(seqs_here, groups, run, width)
    current = (mats_run[:, :, 0], offs_run[:, :, 0])
    mat_list = [current[0]]
    off_list = [current[1]]
    for position in range(1, run):
        current = compose(current, (mats_run[:, :, position], offs_run[:, :, position]))
        mat_list.append(current[0])
        off_list.append(current[1])
    inner_mat = jnp.stack(mat_list, axis=2)
    inner_off = jnp.stack(off_list, axis=2)
    totals = (jnp.moveaxis(current[0], 1, 0), jnp.moveaxis(current[1], 1, 0))
    unit = (
        jnp.broadcast_to(jnp.eye(width, dtype=jnp.float32), (seqs_here, width, width)),
        jnp.zeros((seqs_here, width), jnp.float32),
    )

    def carry_step(carry, item):
        return (compose(carry, item), carry)

    unused, before = lax.scan(carry_step, unit, totals)
    before_mat = jnp.moveaxis(before[0], 0, 1)[:, :, None]
    before_off = jnp.moveaxis(before[1], 0, 1)[:, :, None]
    full_mat, full_off = compose((before_mat, before_off), (inner_mat, inner_off))
    return (
        full_mat.reshape(seqs_here, length, width, width),
        full_off.reshape(seqs_here, length, width),
    )


def per_device(inputs, guess, cotangent, w_input, w_hidden, bias):
    seqs_here, steps_here, width = guess.shape
    tm_count = lax.axis_size("tm")
    incoming = shifted(guess[:, -1:, :], "tm", 1)
    prev = jnp.concatenate([incoming, guess[:, :-1]], axis=1)
    value, parts = cell(inputs, prev, w_input, w_hidden, bias)
    jac = jacobian(prev, w_hidden, *parts)
    shift = value - jnp.einsum("slij,slj->sli", jac, prev, precision=HIGHEST)
    prefix_mat, prefix_off = block_prefix(jac, shift)
    block_mat = prefix_mat[:, -1]
    block_off = prefix_off[:, -1]
    jac_t = jnp.swapaxes(jac, -1, -2)
    identity_mat = jnp.broadcast_to(jnp.eye(width, dtype=jnp.float32), (seqs_here, 1, width, width))
    steps_mat = jnp.flip(jnp.concatenate([jac_t[:, 1:], identity_mat], axis=1), axis=1)
    steps_off = jnp.flip(cotangent, axis=1)
    suffix_mat, suffix_off = block_prefix(steps_mat, steps_off)
    back_mat = jnp.einsum("sij,sjk->sik", jac_t[:, 0], suffix_mat[:, -1], precision=HIGHEST)
    back_off = jnp.einsum("sij,sj->si", jac_t[:, 0], suffix_off[:, -1], precision=HIGHEST)
    zero_state = jnp.zeros((seqs_here, width), jnp.float32)
    unit = (identity_mat[:, 0], zero_state)
    state_in = prefix((block_mat, block_off), "tm", compose, unit, False)[1]
    adjoint_in = prefix((back_mat, back_off), "tm", compose, unit, True)[1]
    new_states = jnp.einsum("slij,sj->sli", prefix_mat, state_in, precision=HIGHEST) + prefix_off
    adjoint = jnp.flip(
        jnp.einsum("slij,sj->sli", suffix_mat, adjoint_in, precision=HIGHEST) + suffix_off, axis=1
    )
    unused, pullback = jax.vjp(
        lambda a, b, c: cell(inputs, prev, a, b, c)[0], w_input, w_hidden, bias
    )
    local_a, local_b, local_c = pullback(adjoint)
    grad_a, grad_b, grad_c = lax.psum((local_a, local_b, local_c), ("seq", "tm"))
    total_steps = lax.axis_size("seq") * seqs_here * tm_count * steps_here
    scale = 1.0 / math.sqrt(total_steps)
    return (new_states, adjoint, grad_a * scale, grad_b * scale, grad_c * scale)


def solution(mesh):
    return jax.shard_map(
        per_device,
        mesh=mesh,
        in_specs=(P("seq", "tm", None), P("seq", "tm", None), P("seq", "tm", None), P(), P(), P()),
        out_specs=(P("seq", "tm", None), P("seq", "tm", None), P(), P(), P()),
        check_vma=False,
    )
```

profile of v0, /device:TPU:0, one launch (start us, length us, event | category | flops | bytes accessed | tf_op | source)
XLA Modules:
  0.0 418.0 jit_solution(681611260634801102)
XLA Ops:
  8.1 2.4 collective-permute-start
  21.6 3.3 copy-done.7
  26.6 4.3 %pad_maximum_fusion = f32[1,256,64,64]{3,2,1,0:T(8,128)} fusion(f32[1,1,64,64]{3,2,1,0:T(8,128)S(1)} %fusion.142, f32[1,255,64,64]{3,2,1,0:T(8,128)S(1)} %slice.381), kind=kLoop, calls=%fused_computation.54 | loop fusion | flops 1048576 | bytes 8388608 | tf_op jit(solution)/shard_map/concatenate | solution.py:117
  30.9 8.4 %rev.17 = f32[1,256,64,64]{3,2,1,0:T(8,128)} reverse(f32[1,256,64,64]{3,2,1,0:T(8,128)} %pad_maximum_fusion), dimensions={1} | reverse | bytes 8388608 | tf_op jit(solution)/shard_map/jit(_flip)/rev | solution.py:117
  80.8 3.3 copy-done.6
  84.2 6.5 %while.61 = (s32[]{:T(128)}, f32[1,64,64]{2,1,0:T(8,128)S(1)}, f32[1,64]{1,0:T(1,128)S(1)}, f32[16,1,64,64]{3,2,1,0:T(8,128)S(1)}, f32[16,1,64]{2,1,0:T(1,128)S(...) while((s32[]{:T(128)}, f32[1,64,64]{2,1,0:T(8,128)S(1)}, ...), condition=%wide.region_5.6_spmd, body=%wide.region_4.5_spmd.sunk | while | flops 3194946 | bytes 216929 | solution.py:94
  90.7 22.0 %fusion.40 = f32[16,1,16,64]{3,1,2,0:T(1,128)S(1)} fusion(f32[16,1,64]{2,1,0:T(1,128)S(1)} %get-tuple-element.273, f32[1,16,16,64,64]{4,3,1,2,0:T(8,128)} %copy-done.6), kind=kOutput, calls=%fused_computation.59 | convolution fusion | flops 12582912 | bytes 4263936 | tf_op jit(solution)/shard_map/...ij,...j->...i/dot_general | solution.py:66
  114.0 14.4 %all-reduce.6 = f32[512]{0:T(512)S(1)} all-reduce(f32[512]{0:T(512)S(1)} %dynamic-update-slice), channel_id=3, replica_groups=mesh['seq'=4,'tm'=8] {'tm'}, use_global_device_ids=true, to_apply=%add.6 | all-reduce | flops 512 | bytes 4096
  128.5 10.3 %fusion.42 = f32[16,16,64,64]{3,2,1,0:T(8,128)S(1)} fusion(f32[16,1,64,64]{3,2,1,0:T(8,128)S(1)} %get-tuple-element.272, f32[1,16,16,64,64]{4,3,1,2,0:T(8,128)} %copy-done.6), kind=kOutput, calls=%fused_computation.61 | convolution fusion | flops 805306368 | bytes 8650752 | tf_op jit(solution)/shard_map/...ij,...jk->...ik/dot_general | solution.py:65
  138.8 3.3 copy-done.9
  143.0 10.4 %all-gather = f32[512,64]{1,0:T(8,128)S(1)} all-gather(f32[64,64]{1,0:T(8,128)S(1)} %fusion.139), channel_id=2, replica_groups=mesh['seq'=4,'tm'=8] {'tm'}, dimensions={0}, use_global_device_ids=true | all-gather | bytes 147456 | tf_op jit(solution)/shard_map/all_gather | solution.py:19
  154.6 5.6 %multiply_reduce_fusion = f32[256,64]{1,0:T(8,128)S(1)} fusion(f32[64,256,64]{0,2,1:T(8,128)} %bitcast.993, f32[64]{0:T(128)S(1)} %bitcast.1113), kind=kLoop, calls=%fused_computation.55 | loop fusion | flops 2080768 | bytes 4260096
  160.7 2.8 multiply_reduce_fusion.2
  165.6 9.4 %multiply_add_fusion = f32[1,16,16,64,64]{4,3,1,2,0:T(8,128)S(1)} fusion(f32[64,64]{1,0:T(8,128)S(1)} %fusion.140, f32[16,16,64]{2,0,1:T(8,128)S(1)} %copy.333, f32[64,64]{1,0:T(8,128)S(1)} %copy.331, f32[16,16,64]{2,0,1:T(8,128)S(1)} %copy.330, f32[64,64]{1,0:T(8,128)S(1)} %copy.328, f32[16,16,64]{2,0,1:T(8,128)S(1)} %copy.327, f32[64,64]{1,0:T(8,128)S(1)} %copy.325, ...), kind=kLoop, calls=%fused_computation.58 | loop fusion | flops 7340032 | bytes 4521984 | tf_op jit(solution)/shard_map/add | solution.py:57
  182.4 2.4 fusion.60
  217.7 3.3 copy-done.4
  221.1 6.5 %while.60 = (s32[]{:T(128)}, f32[1,64,64]{2,1,0:T(8,128)S(1)}, f32[1,64]{1,0:T(1,128)S(1)}, f32[16,1,64,64]{3,2,1,0:T(8,128)S(1)}, f32[16,1,64]{2,1,0:T(1,128)S(...) while((s32[]{:T(128)}, f32[1,64,64]{2,1,0:T(8,128)S(1)}, ...), condition=%wide.region_1.2_spmd, body=%wide.region_0.1_spmd.sunk | while | flops 3194946 | bytes 216929 | solution.py:94
  227.6 22.0 %fusion.44 = f32[16,1,16,64]{3,1,2,0:T(1,128)S(1)} fusion(f32[16,1,64]{2,1,0:T(1,128)S(1)} %get-tuple-element.270, f32[1,16,16,64,64]{4,3,1,2,0:T(8,128)} %copy-done.4), kind=kOutput, calls=%fused_computation.63 | convolution fusion | flops 12582912 | bytes 4263936 | tf_op jit(solution)/shard_map/...ij,...j->...i/dot_general | solution.py:66
  249.7 7.8 %all_gather.19 = f32[8,1,64]{2,1,0:T(1,128)S(1)} all-gather(f32[1,1,64]{2,1,0:T(1,128)S(1)} %slice.380), channel_id=1, replica_groups=mesh['seq'=4,'tm'=8] {'tm'}, dimensions={0}, use_global_device_ids=true | all-gather | bytes 2304 | tf_op jit(solution)/shard_map/all_gather | solution.py:19
  257.5 8.4 %fusion.46 = f32[16,16,64,64]{3,2,1,0:T(8,128)S(1)} fusion(f32[16,1,64,64]{3,2,1,0:T(8,128)S(1)} %get-tuple-element.269, f32[1,16,16,64,64]{4,3,1,2,0:T(8,128)S(1)} %copy-done.5), kind=kOutput, calls=%fused_computation.65 | convolution fusion | flops 805306368 | bytes 8650752 | tf_op jit(solution)/shard_map/...ij,...jk->...ik/dot_general | solution.py:65
  266.0 3.3 copy-done.8
  269.3 9.5 %all_gather.18 = f32[8,1,64,64]{3,2,1,0:T(8,128)S(1)} all-gather(f32[1,1,64,64]{3,2,1,0:T(8,128)S(1)} %slice.379), channel_id=1, replica_groups=mesh['seq'=4,'tm'=8] {'tm'}, dimensions={0}, use_global_device_ids=true | all-gather | bytes 147456 | tf_op jit(solution)/shard_map/all_gather | solution.py:19
  280.7 5.6 %multiply_reduce_fusion.1 = f32[256,64]{1,0:T(8,128)S(1)} fusion(f32[64,256,64]{0,2,1:T(8,128)} %bitcast.991, f32[64]{0:T(128)S(1)} %bitcast.1112), kind=kLoop, calls=%fused_computation.56 | loop fusion | flops 2080768 | bytes 4260096 | tf_op jit(solution)/shard_map/slij,sj->sli/dot_general | solution.py:126
  287.1 121.1 %all-reduce.10.cloned.1.call-done = (f32[64,192]{1,0:T(8,128)}, f32[64,192]{1,0:T(8,128)}, f32[256]{0:T(256)}) async-done(((f32[64,192]{1,0:T(8,128)}, f32[64,192]{1,0:T(8,128)}, f32[256]{0:T(256)}), (f32[64,192]{1,0:T(8,128)}, f32[64,192]{1,0:T(8,128)}, f32[256]{0:T(256)})) %all-reduce.10.cloned.1.call-update) | async-done | bytes 99344 | tf_op jit(solution)/shard_map/psum | solution.py:134
  (412 shorter events, 120.3 us)
Async XLA Ops:
  7.2 7.3 %copy-start = (f32[1,256,64]{1,2,0:T(8,128)S(1)}, f32[1,256,64]{1,2,0:T(8,128)}, u32[]{:S(2)}) copy-start(f32[1,256,64]{1,2,0:T(8,128)} %param.14) | copy-start | bytes 196612
  7.2 401.0 %all-reduce.10.cloned.1.call-start = ((), (), s32[]{:S(2)}) async-start(), calls=%async_computation | async-start | bytes 264192 | tf_op jit(solution)/shard_map/psum | solution.py:134
  8.1 9.6 %collective-permute-start = (f32[1,1,64]{1,2,0:T(8,128)S(1)}, f32[1,1,64]{1,2,0:T(8,128)S(1)}, u32[]{:S(2)}, u32[]{:S(2)}) collective-permute-start(f32[1,1,64]{1,2,0:T(8,128)S(1)} %slice.260), channel_id=1, source_target_pairs={{0,1},{1,2},{2,3},{3,4},{4,5},{5,6},{6,7},{8,9},{9,10},{10,11},{11... | collective-permute-start | bytes 776 | tf_op jit(solution)/shard_map/ppermute | solution.py:14
  11.3 15.3 %copy-start.10 = (f32[1,64,64]{2,1,0:T(8,128)}, f32[1,64,64]{2,1,0:T(8,128)S(1)}, u32[]{:S(2)}) copy-start(f32[1,64,64]{2,1,0:T(8,128)S(1)} %fusion.141) | copy-start | bytes 49156
  21.6 3.3 copy-start.7
  39.2 31.4 %copy-start.3 = (f32[1,256,64,64]{3,2,1,0:T(8,128)S(1)}, f32[1,256,64,64]{3,2,1,0:T(8,128)}, u32[]{:S(2)}) copy-start(f32[1,256,64,64]{3,2,1,0:T(8,128)} %rev.17) | copy-start | bytes 12582916
  75.6 8.6 %copy-start.12 = (f32[1,64,64]{2,1,0:T(8,128)S(1)}, f32[1,64,64]{2,1,0:T(8,128)}, u32[]{:S(2)}) copy-start(f32[1,64,64]{2,1,0:T(8,128)} %copy-done.10) | copy-start | bytes 49156
  80.8 3.3 copy-start.6
  138.8 3.3 copy-start.9
  160.7 24.1 %copy-start.13 = (f32[256,64]{0,1:T(8,128)}, f32[256,64]{0,1:T(8,128)S(1)}, u32[]{:S(2)}) copy-start(f32[256,64]{0,1:T(8,128)S(1)} %reverse.3) | copy-start | bytes 196612
  174.9 3.3 copy-start.1
  180.2 28.2 %copy-start.2 = (f32[1,16,16,64,64]{4,3,1,2,0:T(8,128)S(1)}, f32[1,16,16,64,64]{4,3,1,2,0:T(8,128)}, u32[]{:S(2)}) copy-start(f32[1,16,16,64,64]{4,3,1,2,0:T(8,128)} %copy-done.1) | copy-start | bytes 12582916
  212.5 8.6 %copy-start.11 = (f32[1,64,64]{2,1,0:T(8,128)S(1)}, f32[1,64,64]{2,1,0:T(8,128)}, u32[]{:S(2)}) copy-start(f32[1,64,64]{2,1,0:T(8,128)} %copy-done.10) | copy-start | bytes 49156
  217.7 3.3 copy-start.4
  227.6 29.9 %copy-start.5 = (f32[1,16,16,64,64]{4,3,1,2,0:T(8,128)S(1)}, f32[1,16,16,64,64]{4,3,1,2,0:T(8,128)}, u32[]{:S(2)}) copy-start(f32[1,16,16,64,64]{4,3,1,2,0:T(8,128)} %copy-done.4) | copy-start | bytes 12582916
  266.0 3.3 copy-start.8
Sparse Core Ops, SparseCore 0:
  286.5 121.6 all-reduce.9
where the time goes:
time: 424 us; the launch traced here: 418 us
  matrix products  162 us (38%)
  waiting for transfers between devices  121 us (29%)
  blocking collectives  42 us (10%)
  local copies, waits for them, and re-layouts  39.2 us (9%)
  other arithmetic  34.2 us (8%)
  between operations  15.8 us (4%)
    psum x1, waiting for transfers between devices, per_device(): lax.psum((local_a, local_b, local_c), ('seq', 'tm'))  121 us
    dot_general x78, matrix products, compose(): jnp.einsum('...ij,...j->...i', later[0], earlier[1], precision=HIGHEST)  110 us
    dot_general x64, matrix products, compose(): jnp.einsum('...ij,...jk->...ik', later[0], earlier[0], precision=HIGHEST)  45 us
    all_gather x3, blocking collectives, prefix(): pieces = jax.tree.map(lambda part: lax.all_gather(part, axis), value)  27.6 us
    unnamed x37, local copies, waits for them, and re-layouts  22 us
    unnamed x1, blocking collectives  14.4 us
    add x1, other arithmetic, jacobian(): coef_cand[..., :, None] * w_cand + coef_reset[..., :, None] * w_reset  9.37 us
  transfers between devices with their start and end apart: 2, of which 1 were waited for; matrix products, arithmetic and copies ran while one was open for 2% of the time, Pallas kernels for 0%

commit v1 on v0

v1 whole, which is shorter than its diff:
```python
import functools
import math

import jax
import jax.numpy as jnp
from jax import lax
from jax.experimental import pallas as pl
from jax.experimental.pallas import tpu as pltpu
from jax.sharding import PartitionSpec as P

HIGHEST = lax.Precision.HIGHEST
MESH = pl.DeviceIdType.MESH
F32 = jnp.float32
BF16 = jnp.bfloat16
RUN = 16


def dot(a, b):
    return jnp.dot(a, b, precision=HIGHEST, preferred_element_type=F32)


def dot_t(a, b):
    return lax.dot_general(
        a, b, (((1,), (1,)), ((), ())), precision=HIGHEST, preferred_element_type=F32
    )


def split(x):
    high = x.astype(BF16)
    return high, (x - high.astype(F32)).astype(BF16)


def pack(x):
    half = x.shape[0] // 2
    return jnp.concatenate([x[:half], x[half:]], axis=1)


def twice(w):
    zero = jnp.zeros_like(w)
    return jnp.concatenate(
        [jnp.concatenate([w, zero], axis=1), jnp.concatenate([zero, w], axis=1)], axis=0
    )


def join(early, late):
    a0, b0, c0 = early
    a1, b1, c1 = late
    return (dot(a0, a1), dot(b0, a1) + b1, dot_t(c1, a0) + c0)


def body(
    tm, seq, scale,
    x_ref, g_ref, c_ref, wi_ref, wh_ref, b_ref,
    ns_ref, adj_ref, gi_ref, gh_ref, gb_ref,
    halo, p_s, q_s, w_s, u_s, s_s, c_s, sq_s, lam_s, new_s, lhs_s,
    wh2_s, wl_s, wt_s, mat_s, off_s, acc_s, maps, grad_s, rs_s, seq_s, full_s,
    h_send, h_recv, m_send, m_recv, r_send, r_recv, q_send, q_recv, f_send, f_recv,
):
    me, my_seq = lax.axis_index("tm"), lax.axis_index("seq")
    steps, width = x_ref.shape[1], x_ref.shape[2]
    rows = steps // 2
    pairs = rows // RUN

    def peer(k):
        return lax.rem(me + k, tm)

    def seq_peer(k):
        return lax.rem(my_seq + k, seq)

    barrier = pltpu.get_barrier_semaphore()
    for k in range(1, tm):
        pl.semaphore_signal(barrier, inc=1, device_id=(my_seq, peer(k)), device_id_type=MESH)
    for k in range(1, seq):
        pl.semaphore_signal(barrier, inc=1, device_id=(seq_peer(k), me), device_id_type=MESH)

    guess = g_ref[0]
    halo[0] = jnp.concatenate([guess[steps - 8 :], guess[steps - 8 :]], axis=1)
    pl.semaphore_wait(barrier, tm + seq - 2)
    halo_copy = pltpu.make_async_remote_copy(
        halo.at[0], halo.at[1], h_send, h_recv, device_id=(my_seq, peer(1)), device_id_type=MESH
    )
    halo_copy.start()

    x = x_ref[0]
    wi, wh = wi_ref[...], wh_ref[...]

    def gates(w):
        return (w[:, 2 * width :], w[:, :width], w[:, width : 2 * width])

    big_i = jnp.concatenate([twice(w) for w in gates(wi)], axis=1)
    big_h = jnp.concatenate([twice(w) for w in gates(wh)], axis=1)
    high, low = split(big_h)
    wh2_s[...] = jnp.concatenate([high, high], axis=0)
    wl_s[...] = low
    back = jnp.concatenate([twice(w.T) for w in gates(wh)], axis=0)
    high, low = split(back)
    wt_s[...] = jnp.concatenate([high, low], axis=1)
    bias = b_ref[...]

    def bias_of(i):
        piece = bias[:, i * width : (i + 1) * width]
        return jnp.concatenate([piece, piece], axis=1)

    c_s[...] = pack(c_ref[0])
    gi = dot(pack(x), big_i)
    two = 2 * width

    halo_copy.wait()
    first = jnp.where(me > 0, halo[1][7:8, :width], 0.0)
    prev_full = jnp.concatenate([first, guess[: steps - 1]], axis=0)
    prev = pack(prev_full)
    lhs_s[...] = jnp.concatenate([x, prev_full], axis=1).T
    gh = dot(prev, big_h)
    ghn, ghr, ghz = gh[:, :two], gh[:, two : 2 * two], gh[:, 2 * two :]
    reset = jax.nn.sigmoid(gi[:, two : 2 * two] + bias_of(0) + ghr)
    update = jax.nn.sigmoid(gi[:, 2 * two :] + bias_of(1) + ghz)
    hsum = ghn + bias_of(3)
    cand = jnp.tanh(gi[:, :two] + bias_of(2) + reset * hsum)
    keep = 1.0 - update
    squash = keep * (1.0 - cand * cand)
    coef_p = squash * reset
    coef_q = coef_p * hsum * (1.0 - reset)
    coef_w = (prev - cand) * update * keep
    p_s[...], q_s[...], w_s[...], u_s[...], sq_s[...] = coef_p, coef_q, coef_w, update, squash
    s_s[...] = keep * cand - (coef_p * ghn + coef_q * ghr + coef_w * ghz)

    def at(ref, s):
        return ref[pl.ds(s, pairs, stride=RUN), :]

    def forward_dot(z):
        high, low = split(z)
        both = jnp.concatenate([high, low], axis=1)
        return jnp.dot(both, wh2_s[...], preferred_element_type=F32) + jnp.dot(
            high, wl_s[...], preferred_element_type=F32
        )

    eye = (
        lax.broadcasted_iota(jnp.int32, (width, two), 0)
        == lax.rem(lax.broadcasted_iota(jnp.int32, (width, two), 1), width)
    ).astype(F32)
    mat_s[...] = jnp.broadcast_to(eye[None], (pairs, width, two)).reshape(pairs * width, two)
    off_s[...] = jnp.zeros_like(off_s)
    acc_s[...] = jnp.zeros_like(acc_s)

    def group_step(s, carry):
        p, q, w, u = at(p_s, s), at(q_s, s), at(w_s, s), at(u_s, s)
        old = mat_s[...]
        y = forward_dot(old)
        shape = (pairs, width, two)
        new = (
            p[:, None, :] * y[:, :two].reshape(shape)
            + q[:, None, :] * y[:, two : 2 * two].reshape(shape)
            + w[:, None, :] * y[:, 2 * two :].reshape(shape)
            + u[:, None, :] * old.reshape(shape)
        )
        mat_s[...] = new.reshape(pairs * width, two)
        acc_s[...] += (new * at(c_s, s)[:, None, :]).reshape(pairs * width, two)
        off_s[...] = forward_vector(s, off_s[...])
        return carry

    def forward_vector(s, z):
        y = forward_dot(z)
        return (
            at(p_s, s) * y[:, :two]
            + at(q_s, s) * y[:, two : 2 * two]
            + at(w_s, s) * y[:, 2 * two :]
            + at(u_s, s) * z
            + at(s_s, s)
        )

    lax.fori_loop(0, RUN, group_step, 0)

    lane = lax.broadcasted_iota(jnp.int32, (width, two), 1)
    zeros = jnp.zeros((width, two), F32)

    def blocks(z):
        return jnp.concatenate(
            [jnp.where(lane < width, z, 0.0), jnp.where(lane < width, 0.0, z)], axis=0
        )

    def turn(z):
        return pltpu.roll(z, width, 1)

    def lower(z):
        return jnp.where(lane[: z.shape[0]] < width, z, 0.0)

    ones = jnp.ones((8, two), F32)
    level = []
    for j in range(pairs):
        rows_j = slice(j * width, (j + 1) * width)
        level.append((
            blocks(mat_s[rows_j, :]),
            jnp.broadcast_to(off_s[j : j + 1, :], (8, two)),
            dot_t(ones, blocks(acc_s[rows_j, :])),
        ))
    tree = [level]
    while len(level) > 1:
        level = [join(level[i], level[i + 1]) for i in range(0, len(level), 2)]
        tree.append(level)
    mat, off, coff = level[0]
    first_half = (jnp.concatenate([mat[:width], zeros], axis=0), lower(off), lower(coff))
    last_half = (
        jnp.concatenate([turn(mat[width:]), zeros], axis=0), lower(turn(off)), lower(turn(coff))
    )
    total, off, coff = join(first_half, last_half)
    half = width // 2
    maps[me] = jnp.concatenate(
        [total[:half] + turn(total[half:width]), off + turn(coff)], axis=0
    )
    copies = []
    for k in range(1, tm):
        copy = pltpu.make_async_remote_copy(
            maps.at[me], maps.at[me], m_send.at[k], m_recv.at[k],
            device_id=(my_seq, peer(k)), device_id_type=MESH,
        )
        copy.start()
        copies.append(copy)
    for copy in copies:
        copy.wait()

    def chain(d, carry):
        state, adj = carry
        other = tm - 1 - d

        def load(i):
            block = maps[i]
            mat = block[:half]
            mat = jnp.concatenate([lower(mat), lower(turn(mat)), zeros], axis=0)
            return mat, lower(block[half:]), lower(turn(block[half:]))

        mat, off, unused = load(d)
        state = jnp.where(d < me, dot(state, mat) + off, state)
        mat, unused, coff = load(other)
        adj = jnp.where(other > me, dot_t(adj, mat) + coff, adj)
        return state, adj

    zero = jnp.zeros((8, two), F32)
    state_in, adj_in = lax.fori_loop(0, tm, chain, (zero, zero))

    states = [state_in + turn(dot(state_in, first_half[0]) + first_half[1])]
    adjs = [dot_t(adj_in, last_half[0]) + last_half[2] + turn(adj_in)]
    for level in tree[-2::-1]:
        next_states, next_adjs = [], []
        for i in range(len(states)):
            (a0, b0, unused), (a1, unused, c1) = level[2 * i], level[2 * i + 1]
            next_states += [states[i], dot(states[i], a0) + b0]
            next_adjs += [dot_t(adjs[i], a1) + c1, adjs[i]]
        states, adjs = next_states, next_adjs

    def rows_of(parts):
        return jnp.concatenate([part[:1] for part in parts], axis=0)

    def adjoint_step(i, carry):
        s = RUN - 1 - i
        lam = at(c_s, s) + carry
        lam_s[pl.ds(s, pairs, stride=RUN), :] = lam
        d = jnp.concatenate([at(p_s, s) * lam, at(q_s, s) * lam, at(w_s, s) * lam], axis=1)
        d = jnp.concatenate([d, d], axis=0)
        low = d - d.astype(BF16).astype(F32)
        upper = lax.broadcasted_iota(jnp.int32, d.shape, 0) < pairs
        both = jnp.where(upper, d, low).astype(BF16)
        y = jnp.dot(both, wt_s[...], preferred_element_type=F32)
        return at(u_s, s) * lam + y[:pairs, :two] + y[:pairs, two:] + y[pairs:, :two]

    lax.fori_loop(0, RUN, adjoint_step, rows_of(adjs))

    lam = lam_s[...]
    adj_ref[0] = jnp.concatenate([lam[:, :width], lam[:, width:]], axis=0)
    parts = [q_s[...] * lam, w_s[...] * lam, sq_s[...] * lam, p_s[...] * lam]
    terms = jnp.concatenate(
        [
            jnp.concatenate([part[:, :width] for part in parts], axis=1),
            jnp.concatenate([part[:, width:] for part in parts], axis=1),
        ],
        axis=0,
    )
    grads = dot(lhs_s[...], terms)
    sums = jnp.sum(terms, axis=0, keepdims=True)
    grad_s[:two] = grads[:, :two]
    grad_s[two:] = grads[:, two:]
    row = lax.broadcasted_iota(jnp.int32, (8, width), 0)
    block = jnp.zeros((8, width), F32)
    for i in range(4):
        block = jnp.where(row == i, sums[:, i * width : (i + 1) * width], block)
    grad_s[two : two + 8, width:] = block

    piece = grad_s.shape[0] // tm
    copies = []
    for k in range(1, tm):
        copy = pltpu.make_async_remote_copy(
            grad_s.at[pl.ds(pl.multiple_of(peer(k) * piece, 8), piece)], rs_s.at[k],
            r_send.at[k], r_recv.at[k], device_id=(my_seq, peer(k)), device_id_type=MESH,
        )
        copy.start()
        copies.append(copy)

    def state_step(s, z):
        z = forward_vector(s, z)
        new_s[pl.ds(s, pairs, stride=RUN), :] = z
        return z

    lax.fori_loop(0, RUN, state_step, rows_of(states))
    new = new_s[...]
    ns_ref[0] = jnp.concatenate([new[:, :width], new[:, width:]], axis=0)

    for copy in copies:
        copy.wait()
    part = grad_s[pl.ds(pl.multiple_of(me * piece, 8), piece)]
    for k in range(1, tm):
        part = part + rs_s[k]
    seq_s[my_seq] = part
    copies = []
    for k in range(1, seq):
        copy = pltpu.make_async_remote_copy(
            seq_s.at[my_seq], seq_s.at[my_seq], q_send.at[k], q_recv.at[k],
            device_id=(seq_peer(k), me), device_id_type=MESH,
        )
        copy.start()
        copies.append(copy)
    for copy in copies:
        copy.wait()
    part = seq_s[0]
    for k in range(1, seq):
        part = part + seq_s[k]
    full_s[me] = part * scale
    copies = []
    for k in range(1, tm):
        copy = pltpu.make_async_remote_copy(
            full_s.at[me], full_s.at[me], f_send.at[k], f_recv.at[k],
            device_id=(my_seq, peer(k)), device_id_type=MESH,
        )
        copy.start()
        copies.append(copy)
    for copy in copies:
        copy.wait()
    whole = full_s[...].reshape(2 * two, two)
    gi_ref[...] = jnp.concatenate([whole[:width], whole[two : two + width, :width]], axis=1)
    gh_ref[...] = jnp.concatenate([whole[width:two], whole[two + width :, width:]], axis=1)
    gb_ref[...] = jnp.concatenate(
        [whole[two + i : two + i + 1, width:] for i in range(4)], axis=1
    )


def per_device(tm, seq, inputs, guess, cotangent, w_input, w_hidden, bias):
    unused, steps, width = guess.shape
    two = 2 * width
    rows = steps // 2
    pairs = rows // RUN
    scale = 1.0 / math.sqrt(seq * tm * steps)
    vmem = pltpu.VMEM
    dma = pltpu.SemaphoreType.DMA
    piece = 2 * two // tm
    new, adj, grad_i, grad_h, grad_b = pl.pallas_call(
        functools.partial(body, tm, seq, scale),
        out_shape=(
            jax.ShapeDtypeStruct(guess.shape, F32),
            jax.ShapeDtypeStruct(guess.shape, F32),
            jax.ShapeDtypeStruct(w_input.shape, F32),
            jax.ShapeDtypeStruct(w_hidden.shape, F32),
            jax.ShapeDtypeStruct((1, bias.shape[0]), F32),
        ),
        in_specs=[pl.BlockSpec(memory_space=vmem)] * 6,
        out_specs=(pl.BlockSpec(memory_space=vmem),) * 5,
        scratch_shapes=[
            vmem((2, 8, two), F32),
            *[vmem((rows, two), F32) for unused in range(9)],
            vmem((two, steps), F32),
            vmem((2 * two, 3 * two), BF16),
            vmem((two, 3 * two), BF16),
            vmem((3 * two, 2 * two), BF16),
            vmem((pairs * width, two), F32),
            vmem((pairs, two), F32),
            vmem((pairs * width, two), F32),
            vmem((tm, width // 2 + 8, two), F32),
            vmem((2 * two, two), F32),
            vmem((tm, piece, two), F32),
            vmem((seq, piece, two), F32),
            vmem((tm, piece, two), F32),
            dma, dma,
            dma((tm,)), dma((tm,)),
            dma((tm,)), dma((tm,)),
            dma((seq,)), dma((seq,)),
            dma((tm,)), dma((tm,)),
        ],
        compiler_params=pltpu.CompilerParams(
            collective_id=0, has_side_effects=True, vmem_limit_bytes=32 * 1024 * 1024
        ),
    )(inputs, guess, cotangent, w_input, w_hidden, bias.reshape(1, -1))
    return new, adj, grad_i, grad_h, grad_b.reshape(-1)


def solution(mesh):
    return jax.shard_map(
        functools.partial(per_device, mesh.shape["tm"], mesh.shape["seq"]),
        mesh=mesh,
        in_specs=(P("seq", "tm", None), P("seq", "tm", None), P("seq", "tm", None), P(), P(), P()),
        out_specs=(P("seq", "tm", None), P("seq", "tm", None), P(), P(), P()),
        check_vma=False,
    )
```

time: 424 us -> 45.5 us (0.11); the launches traced: 418 us -> 45.3 us
  matrix products: 162 us -> 0 us
  waiting for transfers between devices: 121 us -> 0 us
  blocking collectives: 42 us -> 0 us
  Pallas kernels: 0 us -> 38.7 us
  other arithmetic: 34.2 us -> 0 us
  local copies, waits for them, and re-layouts: 39.2 us -> 5.91 us
  between operations: 15.8 us -> 0.68 us
    dot_general x148 -> x0, matrix products: 162 us -> none  [the longest x78 110 us: compose(): jnp.einsum('...ij,...j->...i', later[0], earlier[1], precision=HIGHEST)]
    psum x1 -> x0, waiting for transfers between devices: 121 us -> none  [per_device(): lax.psum((local_a, local_b, local_c), ('seq', 'tm'))]
    pallas_call x0 -> x1, Pallas kernels: none -> 38.7 us  [per_device(): pl.pallas_call(functools.partial(body, tm, seq, scale), out_shape=(jax.Sh...]
    all_gather x3 -> x0, blocking collectives: 27.6 us -> none  [prefix(): pieces = jax.tree.map(lambda part: lax.all_gather(part, axis), value)]
    unnamed x37 -> x18, local copies, waits for them, and re-layouts: 22 us -> 5.91 us
    unnamed x1 -> x0, blocking collectives: 14.4 us -> none
    add x5 -> x0, other arithmetic: 9.53 us -> none  [the longest x1 9.37 us: jacobian(): coef_cand[..., :, None] * w_cand + coef_reset[..., :, None] * w_reset]
    rev x4 -> x0, local copies, waits for them, and re-layouts: 8.46 us -> none  [the longest x1 8.35 us: per_device(): jnp.flip(jnp.concatenate([jac_t[:, 1:], identity_mat], axis=1), axis=1)]
  transfers between devices with their start and end apart: 2 -> 0, of which waited for: 1 -> 0; matrix products, arithmetic and copies ran while one was open for 2% -> 0% of each run, Pallas kernels for 0% -> 0%
where the time goes in v1:
time: 45.5 us; the launch traced here: 45.3 us
  Pallas kernels  38.7 us (85%)
  local copies, waits for them, and re-layouts  5.91 us (13%)
  between operations  0.68 us (1%)
    pallas_call x1, Pallas kernels, per_device(): pl.pallas_call(functools.partial(body, tm, seq, scale), out_shape=(jax.Sh...  38.7 us
    unnamed x18, local copies, waits for them, and re-layouts  5.91 us

profile of v1, /device:TPU:0, one launch (start us, length us, event | category | flops | bytes accessed | tf_op | source)
XLA Modules:
  0.0 45.3 jit_solution(15794485668611522476)
XLA Ops:
  0.6 0.0 copy-start.3
  0.6 1.0 %copy.11.x_ref = f32[1,256,64]{2,1,0:T(8,128)S(1)} copy(f32[1,256,64]{1,2,0:T(8,128)} %param.6) | data formatting | bytes 131072 | tf_op args[0]
  1.6 0.0 copy-done.3
  1.6 0.0 copy-start.4
  1.6 0.1 copy.12.g_ref
  1.7 0.7 %copy-done.4 = f32[1,256,64]{1,2,0:T(8,128)S(1)} copy-done((f32[1,256,64]{1,2,0:T(8,128)S(1)}, f32[1,256,64]{1,2,0:T(8,128)}, u32[]{:S(2)}) %copy-start.4) | copy-done | bytes 65560
  2.5 0.0 copy-start
  2.5 0.0 copy-start.1
  2.5 0.0 copy-start.2
  2.5 0.1 copy.13.c_ref
  2.6 0.7 %copy-done = f32[64,192]{1,0:T(8,128)S(1)} copy-done((f32[64,192]{1,0:T(8,128)S(1)}, f32[64,192]{1,0:T(8,128)}, u32[]{:S(2)}) %copy-start) | copy-done | bytes 49176
  3.3 0.0 copy-done.1
  3.3 0.0 copy-done.2
  3.3 38.7 %shard_map.101 = (f32[1,256,64]{2,1,0:T(8,128)S(1)}, f32[1,256,64]{2,1,0:T(8,128)S(1)}, f32[64,192]{1,0:T(8,128)S(1)}, f32[64,192]{1,0:T(8,128)S(1)}, f32[1,256]{1,0:T(1,128)S(1)}) custom-call(f32[1,256,64]{2,1,0:T(8,128)S(1)} %copy.11.x_ref, f32[1,256,64]{2,1,0:T(8,128)S(1)} %copy.12.g_ref, f32[1,256,64]{2,1,0:T(8,128)S(1)} %copy.13.c_ref, ...), custom_call_target="tpu_custom_call" | custom-call | tf_op jit(solution)/shard_map/pallas_call | solution.py:353
  42.0 0.7 %copy.14 = f32[1,256,64]{1,2,0:T(8,128)} copy(f32[1,256,64]{2,1,0:T(8,128)S(1)} %get-tuple-element.15) | data formatting | bytes 131072
  42.7 0.7 %copy.15 = f32[1,256,64]{1,2,0:T(8,128)} copy(f32[1,256,64]{2,1,0:T(8,128)S(1)} %get-tuple-element.16) | data formatting | bytes 131072
  43.4 0.6 %copy.19 = f32[64,192]{1,0:T(8,128)} copy(f32[64,192]{1,0:T(8,128)S(1)} %get-tuple-element.27) | data formatting | bytes 98304
  44.1 0.6 %copy.20 = f32[64,192]{1,0:T(8,128)} copy(f32[64,192]{1,0:T(8,128)S(1)} %get-tuple-element.28) | data formatting | bytes 98304
  44.7 0.6 %copy.21 = f32[256]{0:T(256)} copy(f32[256]{0:T(256)S(1)} %bitcast.3) | data formatting | bytes 2048
Async XLA Ops:
  0.6 1.0 %copy-start.3 = (f32[1,256,64]{1,2,0:T(8,128)S(1)}, f32[1,256,64]{1,2,0:T(8,128)}, u32[]{:S(2)}) copy-start(f32[1,256,64]{1,2,0:T(8,128)} %param.7) | copy-start | bytes 196612
  1.6 0.8 %copy-start.4 = (f32[1,256,64]{1,2,0:T(8,128)S(1)}, f32[1,256,64]{1,2,0:T(8,128)}, u32[]{:S(2)}) copy-start(f32[1,256,64]{1,2,0:T(8,128)} %param.8) | copy-start | bytes 196612
  2.5 0.8 %copy-start = (f32[64,192]{1,0:T(8,128)S(1)}, f32[64,192]{1,0:T(8,128)}, u32[]{:S(2)}) copy-start(f32[64,192]{1,0:T(8,128)} %wi_ref.1) | copy-start | bytes 147460
  2.5 0.9 %copy-start.1 = (f32[64,192]{1,0:T(8,128)S(1)}, f32[64,192]{1,0:T(8,128)}, u32[]{:S(2)}) copy-start(f32[64,192]{1,0:T(8,128)} %wh_ref.1) | copy-start | bytes 147460
  2.5 0.9 %copy-start.2 = (f32[256]{0:T(256)S(1)}, f32[256]{0:T(256)}, u32[]{:S(2)}) copy-start(f32[256]{0:T(256)} %param.11) | copy-start | bytes 3076

commit v2 on v1

--- a/solution.py
+++ b/solution.py
@@ -8,29 +8,35 @@
 from jax.experimental.pallas import tpu as pltpu
 from jax.sharding import PartitionSpec as P
 
-HIGHEST = lax.Precision.HIGHEST
 MESH = pl.DeviceIdType.MESH
 F32 = jnp.float32
 BF16 = jnp.bfloat16
 RUN = 16
 
 
-def dot(a, b):
-    return jnp.dot(a, b, precision=HIGHEST, preferred_element_type=F32)
-
-
-def dot_t(a, b):
-    return lax.dot_general(
-        a, b, (((1,), (1,)), ((), ())), precision=HIGHEST, preferred_element_type=F32
-    )
-
-
 def split(x):
     high = x.astype(BF16)
     return high, (x - high.astype(F32)).astype(BF16)
 
 
+def stack(w):
+    return jnp.concatenate(split(w), axis=0)
+
+
+def mm(a, stacked):
+    both = jnp.concatenate([a, a - a.astype(BF16).astype(F32)], axis=0).astype(BF16)
+    both = jnp.concatenate([both, both], axis=1)
+    y = jnp.dot(both, stacked, preferred_element_type=F32)
+    return y[: a.shape[0]] + y[a.shape[0] :]
+
+
 def pack(x):
+    half = x.shape[1] // 2
+    return jnp.concatenate([x[:, :half], x[:, half:]], axis=0).T
+
+
+def unpack(x):
+    x = x.T
     half = x.shape[0] // 2
     return jnp.concatenate([x[:half], x[half:]], axis=1)
 
@@ -45,19 +51,31 @@
 def join(early, late):
     a0, b0, c0 = early
     a1, b1, c1 = late
-    return (dot(a0, a1), dot(b0, a1) + b1, dot_t(c1, a0) + c0)
+    y = mm(jnp.concatenate([a0, b0], axis=0), stack(a1))
+    count = a0.shape[0]
+    return (y[:count], y[count:] + b1, mm(c1, stack(a0.T)) + c0)
 
 
 def body(
     tm, seq, scale,
-    x_ref, g_ref, c_ref, wi_ref, wh_ref, b_ref,
+    x_hbm, g_hbm, c_hbm, wi_hbm, wh_hbm, b_hbm,
     ns_ref, adj_ref, gi_ref, gh_ref, gb_ref,
+    x_ref, g_ref, c_ref, wi_ref, wh_ref, b_ref, in_sem,
     halo, p_s, q_s, w_s, u_s, s_s, c_s, sq_s, lam_s, new_s, lhs_s,
-    wh2_s, wl_s, wt_s, mat_s, off_s, acc_s, maps, grad_s, rs_s, seq_s, full_s,
+    wh2_s, wt_s, mat_s, off_s, acc_s, maps, grad_s, rs_s, seq_s, full_s,
     h_send, h_recv, m_send, m_recv, r_send, r_recv, q_send, q_recv, f_send, f_recv,
 ):
+    fetch = [
+        pltpu.make_async_copy(source, target, in_sem.at[i])
+        for i, (source, target) in enumerate(
+            [(g_hbm, g_ref), (x_hbm, x_ref), (wi_hbm, wi_ref), (wh_hbm, wh_ref),
+             (b_hbm, b_ref), (c_hbm, c_ref)]
+        )
+    ]
+    for copy in fetch:
+        copy.start()
     me, my_seq = lax.axis_index("tm"), lax.axis_index("seq")
-    steps, width = x_ref.shape[1], x_ref.shape[2]
+    width, steps = x_ref.shape[1], x_ref.shape[2]
     rows = steps // 2
     pairs = rows // RUN
 
@@ -73,25 +91,35 @@
     for k in range(1, seq):
         pl.semaphore_signal(barrier, inc=1, device_id=(seq_peer(k), me), device_id_type=MESH)
 
-    guess = g_ref[0]
-    halo[0] = jnp.concatenate([guess[steps - 8 :], guess[steps - 8 :]], axis=1)
+    fetch[0].wait()
+    guess = pack(g_ref[0])
+    halo[0] = guess[rows - 8 :]
     pl.semaphore_wait(barrier, tm + seq - 2)
     halo_copy = pltpu.make_async_remote_copy(
         halo.at[0], halo.at[1], h_send, h_recv, device_id=(my_seq, peer(1)), device_id_type=MESH
     )
     halo_copy.start()
-
+    for copy in fetch[1:]:
+        copy.wait()
+
+    two = 2 * width
     x = x_ref[0]
     wi, wh = wi_ref[...], wh_ref[...]
+    lane = lax.broadcasted_iota(jnp.int32, (width, two), 1)
+    zeros = jnp.zeros((width, two), F32)
+
+    def turn(z):
+        return pltpu.roll(z, width, 1)
+
+    def lower(z):
+        return jnp.where(lane[: z.shape[0]] < width, z, 0.0)
 
     def gates(w):
         return (w[:, 2 * width :], w[:, :width], w[:, width : 2 * width])
 
     big_i = jnp.concatenate([twice(w) for w in gates(wi)], axis=1)
     big_h = jnp.concatenate([twice(w) for w in gates(wh)], axis=1)
-    high, low = split(big_h)
-    wh2_s[...] = jnp.concatenate([high, high], axis=0)
-    wl_s[...] = low
+    wh2_s[...] = stack(big_h)
     back = jnp.concatenate([twice(w.T) for w in gates(wh)], axis=0)
     high, low = split(back)
     wt_s[...] = jnp.concatenate([high, low], axis=1)
@@ -102,15 +130,14 @@
         return jnp.concatenate([piece, piece], axis=1)
 
     c_s[...] = pack(c_ref[0])
-    gi = dot(pack(x), big_i)
-    two = 2 * width
+    gi = mm(pack(x), stack(big_i))
 
     halo_copy.wait()
-    first = jnp.where(me > 0, halo[1][7:8, :width], 0.0)
-    prev_full = jnp.concatenate([first, guess[: steps - 1]], axis=0)
-    prev = pack(prev_full)
-    lhs_s[...] = jnp.concatenate([x, prev_full], axis=1).T
-    gh = dot(prev, big_h)
+    first = jnp.where(me > 0, lower(turn(halo[1])), 0.0)[7:8]
+    first = first + jnp.where(lane[:1] < width, 0.0, turn(guess[rows - 8 :])[7:8])
+    prev = jnp.concatenate([first, guess[: rows - 1]], axis=0)
+    lhs_s[...] = jnp.concatenate([x, unpack(prev)], axis=0)
+    gh = mm(prev, wh2_s[...])
     ghn, ghr, ghz = gh[:, :two], gh[:, two : 2 * two], gh[:, 2 * two :]
     reset = jax.nn.sigmoid(gi[:, two : 2 * two] + bias_of(0) + ghr)
     update = jax.nn.sigmoid(gi[:, 2 * two :] + bias_of(1) + ghz)
@@ -127,71 +154,73 @@
     def at(ref, s):
         return ref[pl.ds(s, pairs, stride=RUN), :]
 
-    def forward_dot(z):
-        high, low = split(z)
-        both = jnp.concatenate([high, low], axis=1)
-        return jnp.dot(both, wh2_s[...], preferred_element_type=F32) + jnp.dot(
-            high, wl_s[...], preferred_element_type=F32
-        )
-
-    eye = (
-        lax.broadcasted_iota(jnp.int32, (width, two), 0)
-        == lax.rem(lax.broadcasted_iota(jnp.int32, (width, two), 1), width)
-    ).astype(F32)
-    mat_s[...] = jnp.broadcast_to(eye[None], (pairs, width, two)).reshape(pairs * width, two)
-    off_s[...] = jnp.zeros_like(off_s)
-    acc_s[...] = jnp.zeros_like(acc_s)
+    shape = (pairs, width, two)
+    flat = (pairs * width, two)
+    wide = (lane % width == lax.broadcasted_iota(jnp.int32, (width, two), 0)).astype(F32)
+
+    def tiled(w):
+        return jnp.concatenate([w, w], axis=1)[None]
+
+    def mixed(s, yn, yr, yz, old):
+        return (
+            at(p_s, s)[:, None, :] * yn
+            + at(q_s, s)[:, None, :] * yr
+            + at(w_s, s)[:, None, :] * yz
+            + at(u_s, s)[:, None, :] * old
+        )
+
+    first = mixed(0, *[tiled(w) for w in gates(wh)], wide[None])
+    mat_s[0] = first.reshape(flat)
+    acc_s[...] = (first * at(c_s, 0)[:, None, :]).reshape(flat)
+    off_s[0] = at(s_s, 0)
 
     def group_step(s, carry):
-        p, q, w, u = at(p_s, s), at(q_s, s), at(w_s, s), at(u_s, s)
-        old = mat_s[...]
-        y = forward_dot(old)
-        shape = (pairs, width, two)
-        new = (
-            p[:, None, :] * y[:, :two].reshape(shape)
-            + q[:, None, :] * y[:, two : 2 * two].reshape(shape)
-            + w[:, None, :] * y[:, 2 * two :].reshape(shape)
-            + u[:, None, :] * old.reshape(shape)
-        )
-        mat_s[...] = new.reshape(pairs * width, two)
-        acc_s[...] += (new * at(c_s, s)[:, None, :]).reshape(pairs * width, two)
-        off_s[...] = forward_vector(s, off_s[...])
+        old, off = mat_s[s - 1], off_s[s - 1]
+        lhs = jnp.concatenate([old, off, off - off.astype(BF16).astype(F32)], axis=0).astype(BF16)
+        y = jnp.dot(
+            jnp.concatenate([lhs, lhs], axis=1), wh2_s[...], preferred_element_type=F32
+        )
+        mats, offs = y[: pairs * width], y[pairs * width :]
+        offs = offs[:pairs] + offs[pairs:]
+        new = mixed(
+            s,
+            mats[:, :two].reshape(shape),
+            mats[:, two : 2 * two].reshape(shape),
+            mats[:, 2 * two :].reshape(shape),
+            old.reshape(shape),
+        )
+        mat_s[s] = new.reshape(flat)
+        acc_s[...] += (new * at(c_s, s)[:, None, :]).reshape(flat)
+        off_s[s] = (
+            at(p_s, s) * offs[:, :two]
+            + at(q_s, s) * offs[:, two : 2 * two]
+            + at(w_s, s) * offs[:, 2 * two :]
+            + at(u_s, s) * off
+            + at(s_s, s)
+        )
         return carry
 
-    def forward_vector(s, z):
-        y = forward_dot(z)
-        return (
-            at(p_s, s) * y[:, :two]
-            + at(q_s, s) * y[:, two : 2 * two]
-            + at(w_s, s) * y[:, 2 * two :]
-            + at(u_s, s) * z
-            + at(s_s, s)
-        )
-
-    lax.fori_loop(0, RUN, group_step, 0)
-
-    lane = lax.broadcasted_iota(jnp.int32, (width, two), 1)
-    zeros = jnp.zeros((width, two), F32)
+    lax.fori_loop(1, RUN, group_step, 0)
+
+    def spread(z):
+        row = lax.broadcasted_iota(jnp.int32, (2 * two, two), 0) % two // width
+        column = lax.broadcasted_iota(jnp.int32, (2 * two, two), 1) // width
+        ones = (row == column).astype(BF16)
+        return jnp.dot(jnp.concatenate(split(z), axis=1), ones, preferred_element_type=F32)
 
     def blocks(z):
         return jnp.concatenate(
             [jnp.where(lane < width, z, 0.0), jnp.where(lane < width, 0.0, z)], axis=0
         )
 
-    def turn(z):
-        return pltpu.roll(z, width, 1)
-
-    def lower(z):
-        return jnp.where(lane[: z.shape[0]] < width, z, 0.0)
-
-    ones = jnp.ones((8, two), F32)
+    sums = spread(acc_s[...]).reshape(shape) * wide[None]
+    last, last_off = mat_s[RUN - 1], off_s[RUN - 1]
     level = []
     for j in range(pairs):
-        rows_j = slice(j * width, (j + 1) * width)
         level.append((
-            blocks(mat_s[rows_j, :]),
-            jnp.broadcast_to(off_s[j : j + 1, :], (8, two)),
-            dot_t(ones, blocks(acc_s[rows_j, :])),
+            blocks(last[j * width : (j + 1) * width]),
+            jnp.broadcast_to(last_off[j : j + 1], (8, two)),
+            jnp.broadcast_to(jnp.sum(sums[j], axis=0, keepdims=True), (8, two)),
         ))
     tree = [level]
     while len(level) > 1:
@@ -229,22 +258,22 @@
             return mat, lower(block[half:]), lower(turn(block[half:]))
 
         mat, off, unused = load(d)
-        state = jnp.where(d < me, dot(state, mat) + off, state)
+        state = jnp.where(d < me, mm(state, stack(mat)) + off, state)
         mat, unused, coff = load(other)
-        adj = jnp.where(other > me, dot_t(adj, mat) + coff, adj)
+        adj = jnp.where(other > me, mm(adj, stack(mat.T)) + coff, adj)
         return state, adj
 
     zero = jnp.zeros((8, two), F32)
-    state_in, adj_in = lax.fori_loop(0, tm, chain, (zero, zero))
-
-    states = [state_in + turn(dot(state_in, first_half[0]) + first_half[1])]
-    adjs = [dot_t(adj_in, last_half[0]) + last_half[2] + turn(adj_in)]
+    state_in, adj_in = lax.fori_loop(0, tm, chain, (zero, zero), unroll=True)
+
+    states = [state_in + turn(mm(state_in, stack(first_half[0])) + first_half[1])]
+    adjs = [mm(adj_in, stack(last_half[0].T)) + last_half[2] + turn(adj_in)]
     for level in tree[-2::-1]:
         next_states, next_adjs = [], []
         for i in range(len(states)):
             (a0, b0, unused), (a1, unused, c1) = level[2 * i], level[2 * i + 1]
-            next_states += [states[i], dot(states[i], a0) + b0]
-            next_adjs += [dot_t(adjs[i], a1) + c1, adjs[i]]
+            next_states += [states[i], mm(states[i], stack(a0)) + b0]
+            next_adjs += [mm(adjs[i], stack(a1.T)) + c1, adjs[i]]
         states, adjs = next_states, next_adjs
 
     def rows_of(parts):
@@ -265,7 +294,7 @@
     lax.fori_loop(0, RUN, adjoint_step, rows_of(adjs))
 
     lam = lam_s[...]
-    adj_ref[0] = jnp.concatenate([lam[:, :width], lam[:, width:]], axis=0)
+    adj_ref[0] = unpack(lam)
     parts = [q_s[...] * lam, w_s[...] * lam, sq_s[...] * lam, p_s[...] * lam]
     terms = jnp.concatenate(
         [
@@ -274,7 +303,7 @@
         ],
         axis=0,
     )
-    grads = dot(lhs_s[...], terms)
+    grads = mm(lhs_s[...], stack(terms))
     sums = jnp.sum(terms, axis=0, keepdims=True)
     grad_s[:two] = grads[:, :two]
     grad_s[two:] = grads[:, two:]
@@ -294,14 +323,17 @@
         copy.start()
         copies.append(copy)
 
-    def state_step(s, z):
-        z = forward_vector(s, z)
-        new_s[pl.ds(s, pairs, stride=RUN), :] = z
-        return z
-
-    lax.fori_loop(0, RUN, state_step, rows_of(states))
-    new = new_s[...]
-    ns_ref[0] = jnp.concatenate([new[:, :width], new[:, width:]], axis=0)
+    starts = spread(
+        (jnp.concatenate([z[:1][None] for z in states], axis=0) * wide[None]).reshape(flat)
+    ).reshape(shape)
+
+    def state_step(s, carry):
+        moved = jnp.sum(mat_s[s].reshape(shape) * starts, axis=1)
+        new_s[pl.ds(s, pairs, stride=RUN), :] = moved + off_s[s]
+        return carry
+
+    lax.fori_loop(0, RUN, state_step, 0)
+    ns_ref[0] = unpack(new_s[...])
 
     for copy in copies:
         copy.wait()
@@ -341,6 +373,19 @@
     )
 
 
+def finish(a0, a1, a2, a3, a4, b0, b1, b2, b3, b4, sem):
+    copies = [
+        pltpu.make_async_copy(source, target, sem.at[i])
+        for i, (source, target) in enumerate(
+            [(a0, b0), (a1, b1), (a2, b2), (a3, b3), (a4, b4)]
+        )
+    ]
+    for copy in copies:
+        copy.start()
+    for copy in copies:
+        copy.wait()
+
+
 def per_device(tm, seq, inputs, guess, cotangent, w_input, w_hidden, bias):
     unused, steps, width = guess.shape
     two = 2 * width
@@ -350,26 +395,31 @@
     vmem = pltpu.VMEM
     dma = pltpu.SemaphoreType.DMA
     piece = 2 * two // tm
-    new, adj, grad_i, grad_h, grad_b = pl.pallas_call(
+    turned = (guess.shape[0], width, steps)
+    arrays = [jnp.swapaxes(z, 1, 2) for z in (inputs, guess, cotangent)]
+    arrays += [w_input, w_hidden, bias.reshape(1, -1)]
+    outs = (
+        jax.ShapeDtypeStruct(turned, F32),
+        jax.ShapeDtypeStruct(turned, F32),
+        jax.ShapeDtypeStruct(w_input.shape, F32),
+        jax.ShapeDtypeStruct(w_hidden.shape, F32),
+        jax.ShapeDtypeStruct((1, bias.shape[0]), F32),
+    )
+    results = pl.pallas_call(
         functools.partial(body, tm, seq, scale),
-        out_shape=(
-            jax.ShapeDtypeStruct(guess.shape, F32),
-            jax.ShapeDtypeStruct(guess.shape, F32),
-            jax.ShapeDtypeStruct(w_input.shape, F32),
-            jax.ShapeDtypeStruct(w_hidden.shape, F32),
-            jax.ShapeDtypeStruct((1, bias.shape[0]), F32),
-        ),
-        in_specs=[pl.BlockSpec(memory_space=vmem)] * 6,
+        out_shape=outs,
+        in_specs=[pl.BlockSpec(memory_space=pltpu.HBM)] * 6,
         out_specs=(pl.BlockSpec(memory_space=vmem),) * 5,
         scratch_shapes=[
+            *[vmem(z.shape, F32) for z in arrays],
+            dma((6,)),
             vmem((2, 8, two), F32),
             *[vmem((rows, two), F32) for unused in range(9)],
             vmem((two, steps), F32),
             vmem((2 * two, 3 * two), BF16),
-            vmem((two, 3 * two), BF16),
             vmem((3 * two, 2 * two), BF16),
-            vmem((pairs * width, two), F32),
-            vmem((pairs, two), F32),
+            vmem((RUN, pairs * width, two), F32),
+            vmem((RUN, pairs, two), F32),
             vmem((pairs * width, two), F32),
             vmem((tm, width // 2 + 8, two), F32),
             vmem((2 * two, two), F32),
@@ -383,10 +433,17 @@
             dma((tm,)), dma((tm,)),
         ],
         compiler_params=pltpu.CompilerParams(
-            collective_id=0, has_side_effects=True, vmem_limit_bytes=32 * 1024 * 1024
+            collective_id=0, has_side_effects=True, vmem_limit_bytes=48 * 1024 * 1024
         ),
-    )(inputs, guess, cotangent, w_input, w_hidden, bias.reshape(1, -1))
-    return new, adj, grad_i, grad_h, grad_b.reshape(-1)
+    )(*arrays)
+    new, adj, grad_i, grad_h, grad_b = pl.pallas_call(
+        finish,
+        out_shape=outs,
+        in_specs=[pl.BlockSpec(memory_space=vmem)] * 5,
+        out_specs=(pl.BlockSpec(memory_space=pl.ANY),) * 5,
+        scratch_shapes=[dma((5,))],
+    )(*results)
+    return jnp.swapaxes(new, 1, 2), jnp.swapaxes(adj, 1, 2), grad_i, grad_h, grad_b.reshape(-1)
 
 
 def solution(mesh):

time: 45.5 us -> 44 us (0.967)
  Pallas kernels: 38.7 us -> 35 us
  local copies, waits for them, and re-layouts: 5.91 us -> 7.93 us
    pallas_call x1 -> x2, Pallas kernels: 38.7 us -> 35 us  [the longest x1 33.4 us: per_device(): pl.pallas_call(functools.partial(body, tm, seq, scale), out_shape=outs, i...]
    unnamed x18 -> x22, local copies, waits for them, and re-layouts: 5.91 us -> 7.93 us
where the time goes in v2:
time: 44 us; the launch traced here: 43.6 us
  Pallas kernels  35 us (80%)
  local copies, waits for them, and re-layouts  7.93 us (18%)
  between operations  0.67 us (2%)
    pallas_call x1, Pallas kernels, per_device(): pl.pallas_call(functools.partial(body, tm, seq, scale), out_shape=outs, i...  33.4 us
    unnamed x22, local copies, waits for them, and re-layouts  7.93 us
    pallas_call x1, Pallas kernels, per_device(): pl.pallas_call(finish, out_shape=outs, in_specs=[pl.BlockSpec(memory_spac...  1.67 us

profile of v2, /device:TPU:0, one launch (start us, length us, event | category | flops | bytes accessed | tf_op | source)
XLA Modules:
  0.0 43.6 jit_solution(14017878353366641794)
XLA Ops:
  0.6 0.0 copy-start.9
  0.6 0.7 %copy-done.9 = f32[256]{0:T(256)S(1)} copy-done((f32[256]{0:T(256)S(1)}, f32[256]{0:T(256)}, u32[]{:S(2)}) %copy-start.9) | copy-done | bytes 1048
  1.3 0.0 copy-start
  1.3 0.8 %copy-done = f32[1,256,64]{1,2,0:T(8,128)S(1)} copy-done((f32[1,256,64]{1,2,0:T(8,128)S(1)}, f32[1,256,64]{1,2,0:T(8,128)}, u32[]{:S(2)}) %copy-start) | copy-done | bytes 65560
  2.2 0.0 copy-start.1
  2.2 0.8 %copy-done.1 = f32[1,256,64]{1,2,0:T(8,128)S(1)} copy-done((f32[1,256,64]{1,2,0:T(8,128)S(1)}, f32[1,256,64]{1,2,0:T(8,128)}, u32[]{:S(2)}) %copy-start.1) | copy-done | bytes 65560
  3.0 0.0 copy-start.2
  3.0 0.8 %copy-done.2 = f32[1,256,64]{1,2,0:T(8,128)S(1)} copy-done((f32[1,256,64]{1,2,0:T(8,128)S(1)}, f32[1,256,64]{1,2,0:T(8,128)}, u32[]{:S(2)}) %copy-start.2) | copy-done | bytes 65560
  3.8 0.0 copy-start.3
  3.8 0.8 %copy-done.3 = f32[64,192]{1,0:T(8,128)S(1)} copy-done((f32[64,192]{1,0:T(8,128)S(1)}, f32[64,192]{1,0:T(8,128)}, u32[]{:S(2)}) %copy-start.3) | copy-done | bytes 49176
  4.7 0.0 copy-start.4
  4.7 0.8 %copy-done.4 = f32[64,192]{1,0:T(8,128)S(1)} copy-done((f32[64,192]{1,0:T(8,128)S(1)}, f32[64,192]{1,0:T(8,128)}, u32[]{:S(2)}) %copy-start.4) | copy-done | bytes 49176
  5.5 33.4 %shard_map.101 = (f32[1,64,256]{2,1,0:T(8,128)S(1)}, f32[1,64,256]{2,1,0:T(8,128)S(1)}, f32[64,192]{1,0:T(8,128)S(1)}, f32[64,192]{1,0:T(8,128)S(1)}, f32[1,256]{1,0:T(1,128)S(1)}) custom-call(f32[1,64,256]{2,1,0:T(8,128)S(1)} %bitcast.7, f32[1,64,256]{2,1,0:T(8,128)S(1)} %bitcast.8, f32[1,64,256]{2,1,0:T(8,128)S(1)} %bitcast.9, f32[64,192]{1,0:T(8,128)S(1)} %copy-done.3, ...), custom_call_target="tpu_custom_call" | custom-call | tf_op jit(solution)/shard_map/pallas_call | solution.py:408
  38.9 0.0 copy-start.5
  38.9 0.6 %copy-done.5 = f32[1,64,256]{2,1,0:T(8,128)} copy-done((f32[1,64,256]{2,1,0:T(8,128)}, f32[1,64,256]{2,1,0:T(8,128)S(1)}, u32[]{:S(2)}) %copy-start.5) | copy-done | bytes 65560
  39.5 0.0 copy-start.6
  39.5 0.6 %copy-done.6 = f32[1,64,256]{2,1,0:T(8,128)} copy-done((f32[1,64,256]{2,1,0:T(8,128)}, f32[1,64,256]{2,1,0:T(8,128)S(1)}, u32[]{:S(2)}) %copy-start.6) | copy-done | bytes 65560
  40.1 0.0 copy-start.7
  40.1 0.6 %copy-done.7 = f32[64,192]{1,0:T(8,128)} copy-done((f32[64,192]{1,0:T(8,128)}, f32[64,192]{1,0:T(8,128)S(1)}, u32[]{:S(2)}) %copy-start.7) | copy-done | bytes 49176
  40.7 0.0 copy-start.8
  40.7 0.6 %copy-done.8 = f32[64,192]{1,0:T(8,128)} copy-done((f32[64,192]{1,0:T(8,128)}, f32[64,192]{1,0:T(8,128)S(1)}, u32[]{:S(2)}) %copy-start.8) | copy-done | bytes 49176
  41.4 0.0 copy-start.10
  41.4 0.6 %copy-done.10 = f32[1,256]{1,0:T(1,128)} copy-done((f32[1,256]{1,0:T(1,128)}, f32[1,256]{1,0:T(1,128)S(1)}, u32[]{:S(2)}) %copy-start.10) | copy-done | bytes 1048
  42.0 1.7 %shard_map.102 = (f32[1,64,256]{2,1,0:T(8,128)}, f32[1,64,256]{2,1,0:T(8,128)}, f32[64,192]{1,0:T(8,128)}, f32[64,192]{1,0:T(8,128)}, f32[1,256]{1,0:T(1,128)}) custom-call(f32[1,64,256]{2,1,0:T(8,128)} %copy-done.5, f32[1,64,256]{2,1,0:T(8,128)} %copy-done.6, f32[64,192]{1,0:T(8,128)} %copy-done.7, f32[64,192]{1,0:T(8,128)} %copy-done.8, f32[1,256]{1,0:T(1,128)} %copy-done.10), custom_call_target="tpu_custom_call" | custom-call | tf_op jit(solution)/shard_map/pallas_call | solution.py:439
Async XLA Ops:
  0.6 0.7 %copy-start.9 = (f32[256]{0:T(256)S(1)}, f32[256]{0:T(256)}, u32[]{:S(2)}) copy-start(f32[256]{0:T(256)} %param.11) | copy-start | bytes 3076
  1.3 0.8 %copy-start = (f32[1,256,64]{1,2,0:T(8,128)S(1)}, f32[1,256,64]{1,2,0:T(8,128)}, u32[]{:S(2)}) copy-start(f32[1,256,64]{1,2,0:T(8,128)} %param.6) | copy-start | bytes 196612
  2.2 0.8 %copy-start.1 = (f32[1,256,64]{1,2,0:T(8,128)S(1)}, f32[1,256,64]{1,2,0:T(8,128)}, u32[]{:S(2)}) copy-start(f32[1,256,64]{1,2,0:T(8,128)} %param.7) | copy-start | bytes 196612
  3.0 0.8 %copy-start.2 = (f32[1,256,64]{1,2,0:T(8,128)S(1)}, f32[1,256,64]{1,2,0:T(8,128)}, u32[]{:S(2)}) copy-start(f32[1,256,64]{1,2,0:T(8,128)} %param.8) | copy-start | bytes 196612
  3.8 0.8 %copy-start.3 = (f32[64,192]{1,0:T(8,128)S(1)}, f32[64,192]{1,0:T(8,128)}, u32[]{:S(2)}) copy-start(f32[64,192]{1,0:T(8,128)} %wi_hbm.1) | copy-start | bytes 147460
  4.7 0.8 %copy-start.4 = (f32[64,192]{1,0:T(8,128)S(1)}, f32[64,192]{1,0:T(8,128)}, u32[]{:S(2)}) copy-start(f32[64,192]{1,0:T(8,128)} %wh_hbm.1) | copy-start | bytes 147460
  38.9 0.6 %copy-start.5 = (f32[1,64,256]{2,1,0:T(8,128)}, f32[1,64,256]{2,1,0:T(8,128)S(1)}, u32[]{:S(2)}) copy-start(f32[1,64,256]{2,1,0:T(8,128)S(1)} %get-tuple-element.15.a0) | copy-start | bytes 196612
  39.5 0.6 %copy-start.6 = (f32[1,64,256]{2,1,0:T(8,128)}, f32[1,64,256]{2,1,0:T(8,128)S(1)}, u32[]{:S(2)}) copy-start(f32[1,64,256]{2,1,0:T(8,128)S(1)} %get-tuple-element.16.a1) | copy-start | bytes 196612
  40.1 0.6 %copy-start.7 = (f32[64,192]{1,0:T(8,128)}, f32[64,192]{1,0:T(8,128)S(1)}, u32[]{:S(2)}) copy-start(f32[64,192]{1,0:T(8,128)S(1)} %get-tuple-element.17.a2) | copy-start | bytes 147460
  40.7 0.6 %copy-start.8 = (f32[64,192]{1,0:T(8,128)}, f32[64,192]{1,0:T(8,128)S(1)}, u32[]{:S(2)}) copy-start(f32[64,192]{1,0:T(8,128)S(1)} %get-tuple-element.18.a3) | copy-start | bytes 147460
  41.4 0.6 %copy-start.10 = (f32[1,256]{1,0:T(1,128)}, f32[1,256]{1,0:T(1,128)S(1)}, u32[]{:S(2)}) copy-start(f32[1,256]{1,0:T(1,128)S(1)} %get-tuple-element.19.a4) | copy-start | bytes 3076

commit v3 on v2

--- a/solution.py
+++ b/solution.py
@@ -11,7 +11,7 @@
 MESH = pl.DeviceIdType.MESH
 F32 = jnp.float32
 BF16 = jnp.bfloat16
-RUN = 16
+RUN = 8
 
 
 def split(x):
@@ -433,15 +433,16 @@
             dma((tm,)), dma((tm,)),
         ],
         compiler_params=pltpu.CompilerParams(
-            collective_id=0, has_side_effects=True, vmem_limit_bytes=48 * 1024 * 1024
+            collective_id=0, has_side_effects=True, vmem_limit_bytes=64 * 1024 * 1024
         ),
     )(*arrays)
     new, adj, grad_i, grad_h, grad_b = pl.pallas_call(
         finish,
         out_shape=outs,
-        in_specs=[pl.BlockSpec(memory_space=vmem)] * 5,
+        in_specs=[pl.BlockSpec(memory_space=pl.ANY)] * 5,
         out_specs=(pl.BlockSpec(memory_space=pl.ANY),) * 5,
         scratch_shapes=[dma((5,))],
+        compiler_params=pltpu.CompilerParams(vmem_limit_bytes=64 * 1024 * 1024),
     )(*results)
     return jnp.swapaxes(new, 1, 2), jnp.swapaxes(adj, 1, 2), grad_i, grad_h, grad_b.reshape(-1)
 

time: 44 us -> 41.7 us (0.948)
  local copies, waits for them, and re-layouts: 7.93 us -> 0 us
  Pallas kernels: 35 us -> 40.9 us
    unnamed x22 -> x0, local copies, waits for them, and re-layouts: 7.93 us -> none
    pallas_call x1, Pallas kernels: 1.67 us -> 9.12 us  [per_device(): pl.pallas_call(finish, out_shape=outs, in_specs=[pl.BlockSpec(memory_spac...]
    pallas_call x1, Pallas kernels: 33.4 us -> 31.8 us  [per_device(): pl.pallas_call(functools.partial(body, tm, seq, scale), out_shape=outs, i...]
where the time goes in v3:
time: 41.7 us; the launch traced here: 41.5 us
  Pallas kernels  40.9 us (98%)
  between operations  0.64 us (2%)
    pallas_call x1, Pallas kernels, per_device(): pl.pallas_call(functools.partial(body, tm, seq, scale), out_shape=outs, i...  31.8 us
    pallas_call x1, Pallas kernels, per_device(): pl.pallas_call(finish, out_shape=outs, in_specs=[pl.BlockSpec(memory_spac...  9.12 us

profile of v3, /device:TPU:0, one launch (start us, length us, event | category | flops | bytes accessed | tf_op | source)
XLA Modules:
  0.0 41.5 jit_solution(17758641300787629581)
XLA Ops:
  0.6 31.8 %shard_map.101 = (f32[1,64,256]{2,1,0:T(8,128)}, f32[1,64,256]{2,1,0:T(8,128)}, f32[64,192]{1,0:T(8,128)}, f32[64,192]{1,0:T(8,128)}, f32[1,256]{1,0:T(1,128)}) custom-call(f32[1,64,256]{2,1,0:T(8,128)} %bitcast.7, f32[1,64,256]{2,1,0:T(8,128)} %bitcast.8, f32[1,64,256]{2,1,0:T(8,128)} %bitcast.9, f32[64,192]{1,0:T(8,128)} %wi_hbm.1, f32[64,192]{1,0:T(8,128)} %wh_hbm.1, ...), custom_call_target="tpu_custom_call" | custom-call | tf_op jit(solution)/shard_map/pallas_call | solution.py:408
  32.4 9.1 %shard_map.102 = (f32[1,64,256]{2,1,0:T(8,128)}, f32[1,64,256]{2,1,0:T(8,128)}, f32[64,192]{1,0:T(8,128)}, f32[64,192]{1,0:T(8,128)}, f32[1,256]{1,0:T(1,128)}) custom-call(f32[1,64,256]{2,1,0:T(8,128)} %get-tuple-element.15.a0, f32[1,64,256]{2,1,0:T(8,128)} %get-tuple-element.16.a1, f32[64,192]{1,0:T(8,128)} %get-tuple-element.17.a2, ...), custom_call_target="tpu_custom_call" | custom-call | tf_op jit(solution)/shard_map/pallas_call | solution.py:439
